TPU v7x, 512 devices: a whole 4x4x16 slice. The times are simulated.
512 devices in a mesh: ctx: 32 (over y, z_hi, core), fsdp: 16 (over z_lo, x).
Axes of the slice: x: 4, y: 4, z: 16 (z_hi: 4, z_lo: 4; z = z_hi * 4 + z_lo), core: 2. Of those that a mesh axis runs over, the one named last changes fastest.
Arguments:
- events: bfloat16 [8192, 4096], P('ctx'), may hold values from -6 to 6
- tile_mask: int32 [64, 2], P('ctx'), may hold values 0 or 1
- initial_state: float32 [16, 128, 128], P('fsdp'), may hold values from -96 to 96
- w_query: bfloat16 [4096, 2048], P('ctx', 'fsdp'), may hold values from -0.09375 to 0.09375
- w_key: bfloat16 [4096, 2048], P('ctx', 'fsdp'), may hold values from -0.09375 to 0.09375
- w_value: bfloat16 [4096, 2048], P('ctx', 'fsdp'), may hold values from -0.09375 to 0.09375
- cotangent: bfloat16 [8192, 2048], P('ctx', 'fsdp'), may hold values from -6 to 6
Outputs:
- attended: bfloat16 [8192, 2048], P('ctx', 'fsdp')
- events_grad: bfloat16 [8192, 4096], P('ctx')
- query_grad: bfloat16 [4096, 2048], P('ctx', 'fsdp')
- key_grad: bfloat16 [4096, 2048], P('ctx', 'fsdp')
- value_grad: bfloat16 [4096, 2048], P('ctx', 'fsdp')
Inputs may be any that keep to these rules, and one draw needn't show every extreme that they name: `tile_mask`: only entries whose column is not above the row's tile place within its block of 256 events are read.
All inputs are finite; a program needn't handle non-finite values.
Results may differ from a plain program's by a relative error of at most 0.03.
Values may be sent and summed in bfloat16 or wider, within the bound.
No kernel may reach another device: no remote copies, remote signals or barrier semaphores. Data moves between devices by JAX's collectives and lax.ppermute only.
A program may use at most 64 MiB of HBM per device.

v0:
```python
import jax
import jax.numpy as jnp
from jax import lax
from jax.sharding import PartitionSpec as P

HDIM = 128
TILE = 128
epsilon = 1e-06


def prefix(array, axis, combine, identity, reverse):
    count, index = (lax.axis_size(axis), lax.axis_index(axis))
    everything = lax.all_gather(array.astype(jnp.bfloat16), axis)
    start = jnp.broadcast_to(jnp.asarray(identity, array.dtype), array.shape)

    def turn(k, before):
        at = count - 1 - k if reverse else k
        reached = at > index if reverse else at < index
        new = combine(before, everything[at].astype(array.dtype))
        return jnp.where(reached, new, before)

    return lax.fori_loop(0, count, turn, start)


def allowed_pairs(mask_block, tile):
    count = mask_block.shape[0]
    size = count * tile
    row_index = lax.broadcasted_iota(jnp.int32, (size, size), 0)
    col_index = lax.broadcasted_iota(jnp.int32, (size, size), 1)
    tiled = jnp.repeat(jnp.repeat(mask_block, tile, axis=0), tile, axis=1)
    return jnp.where((col_index <= row_index) & (tiled > 0), 1.0, 0.0).astype(jnp.float32)


def add_states(earlier, later):
    return earlier + later


def block_prefix(local_term, reverse):
    return prefix(local_term, "ctx", add_states, jnp.zeros_like(local_term), reverse)


def on_device(events, tile_mask, initial_state, w_query, w_key, w_value, cotangent):
    event_count, head_width = cotangent.shape
    head_count = head_width // HDIM
    stacked = jnp.stack((w_query, w_key, w_value))
    allowed = allowed_pairs(tile_mask, TILE)
    panels = lax.all_gather(stacked, "ctx", axis=1, tiled=True)
    projected = jnp.einsum("td,kdw->ktw", events, panels, preferred_element_type=jnp.float32)
    projected = projected.astype(jnp.bfloat16).reshape(3, event_count, head_count, HDIM)
    queries, key_rows, value_rows = (projected[0], projected[1], projected[2])
    local_state = jnp.einsum(
        "thd,the->hde", key_rows, value_rows, preferred_element_type=jnp.float32
    )
    carried_bf = (block_prefix(local_state, False) + initial_state).astype(jnp.bfloat16)
    scores = (
        jnp.einsum("thd,shd->hts", queries, key_rows, preferred_element_type=jnp.float32)
        * allowed[None]
    )
    mixing = scores.astype(jnp.bfloat16)
    mixture = jnp.einsum("hts,shd->thd", mixing, value_rows, preferred_element_type=jnp.float32)
    mixture = mixture + jnp.einsum(
        "thd,hde->the", queries, carried_bf, preferred_element_type=jnp.float32
    )
    inverse_rms = lax.rsqrt(jnp.mean(mixture * mixture, axis=-1, keepdims=True) + epsilon)
    attended = (mixture * inverse_rms).astype(jnp.bfloat16).reshape(event_count, head_width)
    upstream = cotangent.reshape(event_count, head_count, HDIM).astype(jnp.float32)
    mixture_grad = (
        inverse_rms * upstream
        - mixture * inverse_rms**3 * jnp.mean(upstream * mixture, axis=-1, keepdims=True)
    ).astype(jnp.bfloat16)
    score_grad = (
        jnp.einsum("the,she->hts", mixture_grad, value_rows, preferred_element_type=jnp.float32)
        * allowed[None]
    ).astype(jnp.bfloat16)
    local_grad = jnp.einsum(
        "thd,the->hde", queries, mixture_grad, preferred_element_type=jnp.float32
    )
    later_bf = block_prefix(local_grad, True).astype(jnp.bfloat16)
    query_part = jnp.einsum(
        "hts,shd->thd", score_grad, key_rows, preferred_element_type=jnp.float32
    )
    query_part = query_part + jnp.einsum(
        "the,hde->thd", mixture_grad, carried_bf, preferred_element_type=jnp.float32
    )
    key_part = jnp.einsum("hts,thd->shd", score_grad, queries, preferred_element_type=jnp.float32)
    key_part = key_part + jnp.einsum(
        "she,hde->shd", value_rows, later_bf, preferred_element_type=jnp.float32
    )
    value_part = jnp.einsum(
        "hts,the->she", mixing, mixture_grad, preferred_element_type=jnp.float32
    )
    value_part = value_part + jnp.einsum(
        "shd,hde->she", key_rows, later_bf, preferred_element_type=jnp.float32
    )
    grads = (
        jnp.stack((query_part, key_part, value_part))
        .astype(jnp.bfloat16)
        .reshape(3, event_count, head_width)
    )
    partial_grad = jnp.einsum("ktw,kdw->td", grads, panels, preferred_element_type=jnp.float32)
    events_grad = lax.psum(partial_grad.astype(jnp.bfloat16), "fsdp")
    summed = lax.psum_scatter(
        jnp.einsum("td,ktw->dkw", events, grads, preferred_element_type=jnp.float32).astype(
            jnp.bfloat16
        ),
        "ctx",
        scatter_dimension=0,
        tiled=True,
    )
    return (attended, events_grad, summed[:, 0], summed[:, 1], summed[:, 2])


def solution(mesh):
    placed = (
        P("ctx", None),
        P("ctx", None),
        P("fsdp", None, None),
        P("ctx", "fsdp"),
        P("ctx", "fsdp"),
        P("ctx", "fsdp"),
        P("ctx", "fsdp"),
    )
    return jax.shard_map(
        on_device,
        mesh=mesh,
        in_specs=placed,
        out_specs=(
            P("ctx", "fsdp"),
            P("ctx", None),
            P("ctx", "fsdp"),
            P("ctx", "fsdp"),
            P("ctx", "fsdp"),
        ),
        check_vma=False,
    )
```

profile of v0, /device:TPU:8, one launch (start us, length us, event | category | flops | bytes accessed | tf_op | source)
XLA Modules:
  0.0 613.5 jit_solution(2426722656759367331)
XLA Ops:
  7.2 1.0 copy.38
  8.2 0.9 copy.39
  9.1 0.9 copy.40
  10.8 97.0 %all-gather.6.cloned.1.call-done = bf16[3,4096,128]{1,2,0:T(8,128)(2,1)} async-done(((bf16[3,128,128]{1,2,0:T(8,128)(2,1)}), bf16[3,4096,128]{1,2,0:T(8,128)(2,1)}) %all-gather.6.cloned.1.call-update) | async-done | bytes 3145744 | tf_op jit(solution)/shard_map/all_gather | solution.py:47
  107.8 2.9 fusion.9
  112.3 63.8 %all-gather.8.cloned.1.call-done = bf16[4096,128]{1,0:T(8,128)(2,1)} async-done(((bf16[128,128]{1,0:T(8,128)(2,1)}), bf16[4096,128]{1,0:T(8,128)(2,1)}) %all-gather.8.cloned.1.call-update) | async-done | bytes 1048592 | tf_op jit(solution)/shard_map/all_gather | solution.py:13
  176.0 25.8 %while.30 = (s32[]{:T(128)}, f32[1,128,128]{2,1,0:T(8,128)S(1)}, s32[]{:T(128)}, bf16[32,1,128,128]{3,2,1,0:T(8,128)(2,1)}, s32[]{:T(128)}, /*index=5*/s32[]{:T(128)}) while((s32[]{:T(128)}, f32[1,128,128]{2,1,0:T(8,128)S(1)}, s32[]{:T(128)}, bf16[32,1,128,128]{3,2,1,0:T(8,128)(2,1)}, s32[]{:T(128)}, /*index=5*/s32[]{:T(128)}) %tuple.105), condition=%wide.region_1.2_spmd.clone, body=%wide.region_0.1_spmd.clone.sunk | while | flops 65540 | bytes 163941 | solution.py:22
  176.8 0.8 add_select_fusion.4
  177.7 0.8 add_select_fusion.4
  178.5 0.8 add_select_fusion.4
  179.3 0.8 add_select_fusion.4
  180.1 0.8 add_select_fusion.4
  180.9 0.8 add_select_fusion.4
  181.7 0.8 add_select_fusion.4
  182.5 0.8 add_select_fusion.4
  183.3 0.8 add_select_fusion.4
  184.1 0.8 add_select_fusion.4
  184.9 0.8 add_select_fusion.4
  185.7 0.8 add_select_fusion.4
  186.5 0.8 add_select_fusion.4
  187.3 0.8 add_select_fusion.4
  188.1 0.8 add_select_fusion.4
  188.9 0.8 add_select_fusion.4
  189.7 0.8 add_select_fusion.4
  190.6 0.8 add_select_fusion.4
  191.4 0.8 add_select_fusion.4
  192.2 0.8 add_select_fusion.4
  193.0 0.8 add_select_fusion.4
  193.8 0.8 add_select_fusion.4
  194.6 0.8 add_select_fusion.4
  196.2 0.8 add_select_fusion.4
  200.2 0.8 add_select_fusion.4
  203.8 65.0 %all-gather.10.cloned.1.call-done = bf16[4096,128]{1,0:T(8,128)(2,1)} async-done(((bf16[128,128]{1,0:T(8,128)(2,1)}), bf16[4096,128]{1,0:T(8,128)(2,1)}) %all-gather.10.cloned.1.call-update) | async-done | bytes 1048592 | tf_op jit(solution)/shard_map/all_gather | solution.py:13
  268.8 25.9 %while.31 = (s32[]{:T(128)}, f32[1,128,128]{2,1,0:T(8,128)S(1)}, s32[]{:T(128)}, bf16[32,1,128,128]{3,2,1,0:T(8,128)(2,1)}, s32[]{:T(128)}, /*index=5*/s32[]{:T(128)}, s32[]{:T(128)}, s32[]{:T(128)}) while((s32[]{:T(128)}, f32[1,128,128]{2,1,0:T(8,128)S(1)}, s32[]{:T(128)}, bf16[32,1,128,128]{3,2,1,0:T(8,128)(2,1)}, s32[]{:T(128)}, ...), condition=%wide.region_5.6_spmd.clone, body=%wide.region_4.5_spmd.clone.sunk | while | flops 65544 | bytes 164003 | solution.py:22
  269.6 0.8 add_select_fusion.5
  273.6 0.8 add_select_fusion.5
  276.1 0.8 add_select_fusion.5
  282.5 0.8 add_select_fusion.5
  285.0 0.8 add_select_fusion.5
  289.0 0.8 add_select_fusion.5
  291.5 0.8 add_select_fusion.5
  295.4 2.7 convolution_convert_fusion
  298.1 4.7 copy.56
  302.8 4.5 fusion
  308.1 118.9 %reduce-scatter.4.cloned.1.call-done = bf16[128,384]{1,0:T(8,128)(2,1)} async-done(((bf16[4096,384]{1,0:T(8,128)(2,1)}), bf16[128,384]{1,0:T(8,128)(2,1)}) %reduce-scatter.4.cloned.1.call-update) | async-done | bytes 98320
  427.0 1.0 copy.57
  430.2 173.7 %all-reduce.2.cloned.1.call-done = bf16[256,4096]{1,0:T(8,128)(2,1)} async-done(((bf16[256,4096]{1,0:T(8,128)(2,1)}), bf16[256,4096]{1,0:T(8,128)(2,1)}) %all-reduce.2.cloned.1.call-update) | async-done | bytes 2097168 | tf_op jit(solution)/shard_map/psum | solution.py:101
  603.8 3.1 copy.76
  (80 shorter events, 32.9 us)
Async XLA Ops:
  7.2 100.6 %copy-start = (bf16[256,4096]{1,0:T(8,128)(2,1)S(1)}, bf16[256,4096]{1,0:T(8,128)(2,1)}, u32[]{:S(2)}) copy-start(bf16[256,4096]{1,0:T(8,128)(2,1)} %param.11) | copy-start | bytes 6291460
  7.2 100.6 %all-gather.6.cloned.1.call-start = ((), (), s32[]{:S(2)}) async-start(), calls=%async_computation.1 | async-start | bytes 3244032 | tf_op jit(solution)/shard_map/all_gather | solution.py:47
  10.7 100.9 %copy-start.3 = (s32[2,2]{1,0:T(2,128)S(1)}, s32[2,2]{1,0:T(2,128)}, u32[]{:S(2)}) copy-start(s32[2,2]{1,0:T(2,128)} %param.12) | copy-start | bytes 52
  10.7 101.2 %copy-start.1 = (bf16[256,128]{1,0:T(8,128)(2,1)S(1)}, bf16[256,128]{1,0:T(8,128)(2,1)}, u32[]{:S(2)}) copy-start(bf16[256,128]{1,0:T(8,128)(2,1)} %param.17) | copy-start | bytes 196612
  10.7 191.1 %copy-start.2 = (f32[1,128,128]{2,1,0:T(8,128)S(1)}, f32[1,128,128]{2,1,0:T(8,128)}, u32[]{:S(2)}) copy-start(f32[1,128,128]{2,1,0:T(8,128)} %param.13) | copy-start | bytes 196612
  10.7 165.3 %all-gather.8.cloned.1.call-start = ((), (), s32[]{:S(2)}) async-start(), calls=%async_computation.3 | async-start | bytes 1081344 | tf_op jit(solution)/shard_map/all_gather | solution.py:13
  111.5 157.3 %all-gather.10.cloned.1.call-start = ((), (), s32[]{:S(2)}) async-start(), calls=%async_computation.4 | async-start | bytes 1081344 | tf_op jit(solution)/shard_map/all_gather | solution.py:13
  203.2 223.8 %reduce-scatter.4.cloned.1.call-start = ((), (), s32[]{:S(2)}) async-start(), calls=%async_computation.5 | async-start | bytes 3244032
  302.8 301.1 %all-reduce.2.cloned.1.call-start = ((), (), s32[]{:S(2)}) async-start(), calls=%async_computation.2 | async-start | bytes 4194304 | tf_op jit(solution)/shard_map/psum | solution.py:101
Sparse Core Ops, SparseCore 0:
  11.6 96.0 all-gather.5
  111.6 64.4 all-gather.7
  203.3 65.4 all-gather.9
  302.9 124.0 reduce-scatter.3
  430.6 173.1 all-reduce.1
where the time goes:
time: 618 us; the launch traced here: 613 us
  waiting for transfers between devices  518 us (84%)
  other arithmetic  50.9 us (8%)
  local copies, waits for them, and re-layouts  14.9 us (2%)
  between operations  14 us (2%)
  matrix products  13.5 us (2%)
    psum x1, waiting for transfers between devices, on_device(): events_grad = lax.psum(partial_grad.astype(jnp.bfloat16), 'fsdp')  174 us
    all_gather x2, waiting for transfers between devices, prefix(): everything = lax.all_gather(array.astype(jnp.bfloat16), axis)  129 us
    unnamed x6, waiting for transfers between devices  119 us
    all_gather x1, waiting for transfers between devices, on_device(): panels = lax.all_gather(stacked, 'ctx', axis=1, tiled=True)  97 us
    select_n x64, other arithmetic, turn(): return jnp.where(reached, new, before)  50.1 us
    unnamed x21, local copies, waits for them, and re-layouts  14.7 us
  transfers between devices with their start and end apart: 5, of which 5 were waited for; matrix products, arithmetic and copies ran while one was open for 2% of the time, Pallas kernels for 0%

commit v1 on v0

--- a/solution.py
+++ b/solution.py
@@ -98,7 +98,7 @@
         .reshape(3, event_count, head_width)
     )
     partial_grad = jnp.einsum("ktw,kdw->td", grads, panels, preferred_element_type=jnp.float32)
-    events_grad = lax.psum(partial_grad.astype(jnp.bfloat16), "fsdp")
+    events_grad = jnp.sum(lax.all_gather(partial_grad.astype(jnp.bfloat16), "fsdp"), axis=0)
     summed = lax.psum_scatter(
         jnp.einsum("td,ktw->dkw", events, grads, preferred_element_type=jnp.float32).astype(
             jnp.bfloat16

time: 618 us -> 811 us (1.31)
  the two profiles are of different devices: /device:TPU:8 before, /device:TPU:1 now
where the time goes in v1:
time: 811 us; the launch traced here: 806 us
  waiting for transfers between devices  701 us (86%)
  other arithmetic  63.8 us (8%)
  between operations  14 us (2%)
  matrix products  13.5 us (2%)
  local copies, waits for them, and re-layouts  11.8 us (1%)
    all_gather x1, waiting for transfers between devices, on_device(): lax.all_gather(partial_grad.astype(jnp.bfloat16), 'fsdp')  355 us
    all_gather x2, waiting for transfers between devices, prefix(): everything = lax.all_gather(array.astype(jnp.bfloat16), axis)  130 us
    unnamed x6, waiting for transfers between devices  117 us
    all_gather x1, waiting for transfers between devices, on_device(): panels = lax.all_gather(stacked, 'ctx', axis=1, tiled=True)  98.5 us
    select_n x64, other arithmetic, turn(): return jnp.where(reached, new, before)  50.1 us
  transfers between devices with their start and end apart: 5, of which 5 were waited for; matrix products, arithmetic and copies ran while one was open for 1% of the time, Pallas kernels for 0%

profile of v1, /device:TPU:1, one launch (start us, length us, event | category | flops | bytes accessed | tf_op | source)
XLA Modules:
  0.0 805.9 jit_solution(11901567820254151501)
XLA Ops:
  7.2 1.0 copy.38
  8.2 0.9 copy.39
  9.1 0.9 copy.40
  10.8 98.5 %all-gather.8.cloned.1.call-done = bf16[3,4096,128]{1,2,0:T(8,128)(2,1)} async-done(((bf16[3,128,128]{1,2,0:T(8,128)(2,1)}), bf16[3,4096,128]{1,2,0:T(8,128)(2,1)}) %all-gather.8.cloned.1.call-update) | async-done | bytes 3145744 | tf_op jit(solution)/shard_map/all_gather | solution.py:47
  109.3 2.9 fusion.9
  112.2 0.8 convolution_convert_fusion.2
  113.8 64.9 %all-gather.10.cloned.1.call-done = bf16[4096,128]{1,0:T(8,128)(2,1)} async-done(((bf16[128,128]{1,0:T(8,128)(2,1)}), bf16[4096,128]{1,0:T(8,128)(2,1)}) %all-gather.10.cloned.1.call-update) | async-done | bytes 1048592 | tf_op jit(solution)/shard_map/all_gather | solution.py:13
  178.7 25.8 %while.30 = (s32[]{:T(128)}, f32[1,128,128]{2,1,0:T(8,128)S(1)}, s32[]{:T(128)}, bf16[32,1,128,128]{3,2,1,0:T(8,128)(2,1)}, s32[]{:T(128)}, /*index=5*/s32[]{:T(128)}) while((s32[]{:T(128)}, f32[1,128,128]{2,1,0:T(8,128)S(1)}, s32[]{:T(128)}, bf16[32,1,128,128]{3,2,1,0:T(8,128)(2,1)}, s32[]{:T(128)}, /*index=5*/s32[]{:T(128)}) %tuple.104), condition=%wide.region_1.2_spmd.clone, body=%wide.region_0.1_spmd.clone.sunk | while | flops 65540 | bytes 163933 | solution.py:22
  179.5 0.8 add_select_fusion.4
  180.3 0.8 add_select_fusion.4
  181.1 0.8 add_select_fusion.4
  182.0 0.8 add_select_fusion.4
  182.8 0.8 add_select_fusion.4
  183.6 0.8 add_select_fusion.4
  184.4 0.8 add_select_fusion.4
  185.2 0.8 add_select_fusion.4
  186.0 0.8 add_select_fusion.4
  186.8 0.8 add_select_fusion.4
  187.6 0.8 add_select_fusion.4
  188.4 0.8 add_select_fusion.4
  189.2 0.8 add_select_fusion.4
  190.0 0.8 add_select_fusion.4
  190.8 0.8 add_select_fusion.4
  191.6 0.8 add_select_fusion.4
  192.4 0.8 add_select_fusion.4
  193.2 0.8 add_select_fusion.4
  194.0 0.8 add_select_fusion.4
  194.9 0.8 add_select_fusion.4
  195.7 0.8 add_select_fusion.4
  196.5 0.8 add_select_fusion.4
  198.1 0.8 add_select_fusion.4
  201.3 0.8 add_select_fusion.4
  206.5 65.0 %all-gather.12.cloned.1.call-done = bf16[4096,128]{1,0:T(8,128)(2,1)} async-done(((bf16[128,128]{1,0:T(8,128)(2,1)}), bf16[4096,128]{1,0:T(8,128)(2,1)}) %all-gather.12.cloned.1.call-update) | async-done | bytes 1048592 | tf_op jit(solution)/shard_map/all_gather | solution.py:13
  271.5 26.0 %while.31 = (s32[]{:T(128)}, f32[1,128,128]{2,1,0:T(8,128)S(1)}, s32[]{:T(128)}, bf16[32,1,128,128]{3,2,1,0:T(8,128)(2,1)}, s32[]{:T(128)}, /*index=5*/s32[]{:T(128)}, s32[]{:T(128)}, s32[]{:T(128)}) while((s32[]{:T(128)}, f32[1,128,128]{2,1,0:T(8,128)S(1)}, s32[]{:T(128)}, bf16[32,1,128,128]{3,2,1,0:T(8,128)(2,1)}, s32[]{:T(128)}, ...), condition=%wide.region_5.6_spmd.clone, body=%wide.region_4.5_spmd.clone.sunk | while | flops 65544 | bytes 163995 | solution.py:22
  275.5 0.8 add_select_fusion.5
  277.1 0.8 add_select_fusion.5
  281.2 0.8 add_select_fusion.5
  286.9 0.8 add_select_fusion.5
  291.0 0.8 add_select_fusion.5
  292.6 0.8 add_select_fusion.5
  296.6 0.8 add_select_fusion.5
  298.1 2.7 convolution_convert_fusion
  300.8 4.6 copy.56
  305.5 4.5 fusion
  310.7 117.2 %reduce-scatter.4.cloned.1.call-done = bf16[128,384]{1,0:T(8,128)(2,1)} async-done(((bf16[4096,384]{1,0:T(8,128)(2,1)}), bf16[128,384]{1,0:T(8,128)(2,1)}) %reduce-scatter.4.cloned.1.call-update) | async-done | bytes 98320
  428.0 1.0 copy.57
  431.2 355.2 %all-gather.14.cloned.1.call-done = bf16[4096,4096]{1,0:T(8,128)(2,1)} async-done(((bf16[256,4096]{1,0:T(8,128)(2,1)}), bf16[4096,4096]{1,0:T(8,128)(2,1)}) %all-gather.14.cloned.1.call-update) | async-done | bytes 33554448 | tf_op jit(solution)/shard_map/all_gather | solution.py:101
  786.4 13.0 %reduce_sum.32 = bf16[256,4096]{1,0:T(8,128)(2,1)} reduce(bf16[16,256,4096]{2,1,0:T(8,128)(2,1)} %bitcast.133, bf16[]{:T(256)} %constant.85.clone.1), dimensions={0}, to_apply=%region_6.7 | reduce | flops 15728640 | bytes 35651584 | tf_op jit(solution)/shard_map/reduce_sum | solution.py:101
  (80 shorter events, 32.9 us)
Async XLA Ops:
  7.2 102.1 %copy-start = (bf16[256,4096]{1,0:T(8,128)(2,1)S(1)}, bf16[256,4096]{1,0:T(8,128)(2,1)}, u32[]{:S(2)}) copy-start(bf16[256,4096]{1,0:T(8,128)(2,1)} %param.11) | copy-start | bytes 6291460
  7.2 102.1 %all-gather.8.cloned.1.call-start = ((), (), s32[]{:S(2)}) async-start(), calls=%async_computation.1 | async-start | bytes 3244032 | tf_op jit(solution)/shard_map/all_gather | solution.py:47
  10.7 102.4 %copy-start.3 = (s32[2,2]{1,0:T(2,128)S(1)}, s32[2,2]{1,0:T(2,128)}, u32[]{:S(2)}) copy-start(s32[2,2]{1,0:T(2,128)} %param.12) | copy-start | bytes 52
  10.7 102.8 %copy-start.1 = (bf16[256,128]{1,0:T(8,128)(2,1)S(1)}, bf16[256,128]{1,0:T(8,128)(2,1)}, u32[]{:S(2)}) copy-start(bf16[256,128]{1,0:T(8,128)(2,1)} %param.17) | copy-start | bytes 196612
  10.7 193.8 %copy-start.2 = (f32[1,128,128]{2,1,0:T(8,128)S(1)}, f32[1,128,128]{2,1,0:T(8,128)}, u32[]{:S(2)}) copy-start(f32[1,128,128]{2,1,0:T(8,128)} %param.13) | copy-start | bytes 196612
  10.7 168.0 %all-gather.10.cloned.1.call-start = ((), (), s32[]{:S(2)}) async-start(), calls=%async_computation.2 | async-start | bytes 1081344 | tf_op jit(solution)/shard_map/all_gather | solution.py:13
  113.0 158.4 %all-gather.12.cloned.1.call-start = ((), (), s32[]{:S(2)}) async-start(), calls=%async_computation.3 | async-start | bytes 1081344 | tf_op jit(solution)/shard_map/all_gather | solution.py:13
  205.8 222.1 %reduce-scatter.4.cloned.1.call-start = ((), (), s32[]{:S(2)}) async-start(), calls=%async_computation.5 | async-start | bytes 3244032
  305.4 481.0 %all-gather.14.cloned.1.call-start = ((), (), s32[]{:S(2)}) async-start(), calls=%async_computation.4 | async-start | bytes 35651584 | tf_op jit(solution)/shard_map/all_gather | solution.py:101
Sparse Core Ops, SparseCore 0:
  11.6 97.6 all-gather.7
  113.1 65.5 all-gather.9
  206.0 65.4 all-gather.11
  305.5 122.3 reduce-scatter.3
  430.7 355.6 all-gather.13
